TPU v7x, 32 devices: a whole 2x2x4 slice. The times are simulated.
32 devices in a mesh: rows: 8 (over z, x), cents: 4 (over y, core).
Axes of the slice: x: 2, y: 2, z: 4, core: 2. Of those that a mesh axis runs over, the one named last changes fastest.
Arguments:
- groups: bfloat16 [65536, 1024], P(('rows', 'cents')), may hold values from -60 to 60
- centroids: bfloat16 [65536, 1024], P(('rows', 'cents')), may hold values from -60 to 60
- row_weight: float32 [65536], P(('rows', 'cents')), may hold values from 0.5 to 18
- block_ids: int32 [256, 8], P(('rows', 'cents')), may hold values from 0 to 511, as said below
- block_counts: int32 [256], P(('rows', 'cents')), may hold values from 1 to 8
Outputs:
- centroid_sums: float32 [65536, 1024], P(('rows', 'cents'))
- column_load: float32 [65536], P(('rows', 'cents'))
Inputs may be any that keep to these rules, and one draw needn't show every extreme that they name: `block_ids`: slots k < block_counts[b] are the candidates of row block b; later slots hold valid ids but are unused. List block g is held by the device of index g // 16 in the order rows, then cents. The 8 x 8 slots of the row blocks held by device (r, c) name blocks held by devices (o, c) only, exactly 8 slots for each o, and among those slots exactly 2 distinct blocks of o; the slots of one row block name blocks of distinct holders.
All inputs are finite; a program needn't handle non-finite values.
Results may differ from a plain program's by a relative error of at most 0.0051.
Values may be sent and summed in bfloat16 or wider, within the bound.
A program may use at most 192 MiB of HBM per device.

v0:
```python
import jax
import jax.numpy as jnp
from jax import lax
from jax.sharding import PartitionSpec as P

D = 1024
RB = 256
CB = 128
USE = 2
ITERS = 3


BETA = 32.0
EPSILON = 1e-06
PRIOR = 0.25
HIGHEST = lax.Precision.HIGHEST


def normalize(values):
    widened = values.astype(jnp.float32)
    factor = lax.rsqrt(jnp.mean(widened * widened, axis=-1, keepdims=True) + EPSILON)
    return (widened * factor).astype(jnp.bfloat16)


def routing(block_ids, lists_blocks, cents_count, rows_count, use_count):
    block_total, slots_per_block = block_ids.shape
    pair_count = block_total * slots_per_block
    flat_ids = block_ids.reshape(pair_count)
    holder_row = flat_ids // lists_blocks // cents_count
    local_block = flat_ids % lists_blocks
    pair_index = jnp.arange(pair_count, dtype=jnp.int32)
    same_id = flat_ids[None, :] == flat_ids[:, None]
    first_pair = jnp.min(jnp.where(same_id, pair_index[None, :], pair_count), axis=1)
    is_first = first_pair == pair_index
    earlier_first = (
        is_first[None, :]
        & (holder_row[None, :] == holder_row[:, None])
        & (pair_index[None, :] < pair_index[:, None])
    )
    rank_first = jnp.sum(earlier_first.astype(jnp.int32), axis=1)
    distinct_of_pair = holder_row * use_count + rank_first[first_pair]
    distinct_index = jnp.arange(rows_count * use_count, dtype=jnp.int32)
    chosen = (is_first[None, :] & (distinct_of_pair[None, :] == distinct_index[:, None])).astype(
        jnp.int32
    )
    request_table = jnp.sum(chosen * local_block[None, :], axis=1).reshape(rows_count, use_count)
    pair_onehot = (distinct_of_pair[None, :] == distinct_index[:, None]).astype(jnp.float32)
    dense_of_pair = holder_row * lists_blocks + local_block
    return (distinct_of_pair, request_table, pair_onehot, dense_of_pair)


def holder_onehot(local_in, lists_blocks):
    return (
        local_in.reshape(-1)[None, :] == jnp.arange(lists_blocks, dtype=jnp.int32)[:, None]
    ).astype(jnp.float32)


def body(groups, centroids, row_weight, block_ids, block_counts):
    rows_count = lax.axis_size("rows")
    cents_count = lax.axis_size("cents")
    use_count = USE
    block_total, slots_per_block = block_ids.shape
    lists_blocks = centroids.shape[0] // CB
    rows_norm = normalize(groups).reshape(block_total, RB, D)
    lists_norm = normalize(centroids).reshape(lists_blocks, CB, D)
    weights = row_weight.reshape(block_total, RB)
    weight_sum = lax.psum(jnp.sum(row_weight), ("rows", "cents"))
    target = weight_sum / (lists_blocks * CB * rows_count * cents_count)
    distinct_of_pair, request_table, pair_onehot, dense_of_pair = routing(
        block_ids, lists_blocks, cents_count, rows_count, use_count
    )
    local_in = lax.all_to_all(request_table, "rows", split_axis=0, concat_axis=0, tiled=True)
    owned_map = holder_onehot(local_in, lists_blocks)
    arrived = lax.all_to_all(lists_norm[local_in], "rows", split_axis=0, concat_axis=0, tiled=True)
    picked_lists = arrived.reshape(-1, CB, D)[distinct_of_pair].reshape(
        block_total, slots_per_block, CB, D
    )
    scores = jnp.einsum(
        "brd,bkcd->bkrc", rows_norm, picked_lists, preferred_element_type=jnp.float32
    )
    live_mask = (
        jnp.arange(slots_per_block, dtype=jnp.int32)[None, :] < block_counts[:, None]
    ).astype(jnp.float32)
    kernel = jnp.exp(scores * (BETA / D)) * live_mask[:, :, None, None]
    picked = jnp.ones((block_total, slots_per_block, CB), jnp.float32)
    for iteration in range(ITERS):
        row_sums = jnp.einsum("bkrc,bkc->br", kernel, picked, precision=HIGHEST)
        row_scale = weights / row_sums
        column_parts = jnp.einsum("bkrc,br->bkc", kernel, row_scale, precision=HIGHEST)
        flat_parts = column_parts.reshape(-1, CB)
        outgoing = jnp.dot(pair_onehot, flat_parts, precision=HIGHEST).reshape(
            rows_count, use_count, CB
        )
        incoming = lax.all_to_all(outgoing, "rows", split_axis=0, concat_axis=0, tiled=True)
        column = jnp.dot(owned_map, incoming.reshape(-1, CB), precision=HIGHEST)
        scales = target / (column + PRIOR * target)
        returned = lax.all_to_all(scales[local_in], "rows", split_axis=0, concat_axis=0, tiled=True)
        picked = returned.reshape(-1, CB)[distinct_of_pair].reshape(
            block_total, slots_per_block, CB
        )
    row_sums = jnp.einsum("bkrc,bkc->br", kernel, picked, precision=HIGHEST)
    row_scale = weights / row_sums
    transport = row_scale[:, None, :, None] * kernel * picked[:, :, None, :]
    mass_parts = jnp.dot(
        pair_onehot, jnp.sum(transport, axis=2).reshape(-1, CB), precision=HIGHEST
    ).reshape(rows_count, use_count, CB)
    transport_half = transport.astype(jnp.bfloat16)
    slot_target = distinct_of_pair.reshape(block_total, slots_per_block)
    gathered_sums = jnp.zeros((rows_count * use_count, CB, D), jnp.float32)
    for slot_number in range(slots_per_block):
        slot_part = jnp.einsum(
            "brc,brd->bcd",
            transport_half[:, slot_number],
            rows_norm,
            preferred_element_type=jnp.float32,
        )
        gathered_sums = gathered_sums.at[slot_target[:, slot_number]].add(slot_part)
    got_parts, got_mass = (
        lax.all_to_all(
            gathered_sums.reshape(rows_count, use_count, CB, D),
            "rows",
            split_axis=0,
            concat_axis=0,
            tiled=True,
        ),
        lax.all_to_all(mass_parts, "rows", split_axis=0, concat_axis=0, tiled=True),
    )
    totals = jnp.dot(
        owned_map, got_parts.reshape(rows_count * use_count, CB * D), precision=HIGHEST
    )
    column_mass = jnp.dot(owned_map, got_mass.reshape(-1, CB), precision=HIGHEST)
    return (totals.reshape(-1, D), (column_mass / target).reshape(-1))


def solution(mesh):
    placed = (
        P(("rows", "cents"), None),
        P(("rows", "cents"), None),
        P(("rows", "cents")),
        P(("rows", "cents"), None),
        P(("rows", "cents")),
    )
    return jax.shard_map(
        body,
        mesh=mesh,
        in_specs=placed,
        out_specs=(P(("rows", "cents"), None), P(("rows", "cents"))),
        check_vma=False,
    )
```

profile of v0, /device:TPU:0, one launch (start us, length us, event | category | flops | bytes accessed | tf_op | source)
XLA Modules:
  0.0 615.9 jit_solution(17142766564986375337)
XLA Ops:
  3.4 7.3 %all-to-all-start = ((s32[8,1,2]{2,1,0:T(1,128)}), s32[8,1,2]{2,1,0:T(1,128)S(1)}, u32[]{:S(2)}, u32[]{:S(2)}) async-start(s32[8,1,2]{2,1,0:T(1,128)} %bitcast.2), calls=%async_computation | async-start | bytes 8192 | tf_op jit(solution)/shard_map/all_to_all | solution.py:72
  10.7 3.2 fusion
  14.1 2.8 fusion.1
  17.3 4.9 gather_fusion.1
  22.3 6.2 %all-to-all-start.1 = ((bf16[8,2,128,1024]{3,2,1,0:T(8,128)(2,1)}), bf16[8,2,128,1024]{3,2,1,0:T(8,128)(2,1)}, u32[]{:S(2)}, u32[]{:S(2)}) async-start(bf16[8,2,128,1024]{3,2,1,0:T(8,128)(2,1)} %bitcast.180), calls=%async_computation.1 | async-start | bytes 8388608 | tf_op jit(solution)/shard_map/all_to_all | solution.py:74
  28.7 3.2 fusion.2
  34.7 86.4 %all-to-all-done.1 = bf16[8,2,128,1024]{3,2,1,0:T(8,128)(2,1)} async-done(((bf16[8,2,128,1024]{3,2,1,0:T(8,128)(2,1)}), bf16[8,2,128,1024]{3,2,1,0:T(8,128)(2,1)}, u32[]{:S(2)}, u32[]{:S(2)}) %all-to-all-start.1) | async-done | bytes 4194336 | tf_op jit(solution)/shard_map/all_to_all | solution.py:74
  121.1 9.4 %gather_fusion.2 = bf16[64,128,1024]{2,1,0:T(8,128)(2,1)} fusion(bf16[16,128,1024]{2,1,0:T(8,128)(2,1)} %bitcast.6, s32[1024]{0:T(1024)S(1)} %pad_clamp_fusion), kind=kCustom, calls=%fused_computation.2 | custom fusion | bytes 33554688 | tf_op jit(solution)/shard_map/gather | solution.py:75
  130.5 15.1 %exponential_multiply_fusion = f32[8,8,128,256]{3,2,1,0:T(8,128)} fusion(f32[8,8]{1,0:T(8,128)S(1)} %fusion.78, bf16[8,8,128,1024]{3,2,1,0:T(8,128)(2,1)} %bitcast.178, bf16[8,256,1024,1]{2,1,3,0:T(8,128)(2,1)} %bitcast.167), kind=kOutput, calls=%fused_computation.41 | convolution fusion | flops 4299161600 | bytes 29360384 | tf_op jit(solution)/shard_map/brd,bkcd->bkrc/dot_general | solution.py:78
  145.6 7.8 %fusion.16 = f32[8,1,256,1]{2,1,3,0:T(1,128)S(1)} fusion(f32[8,8,128,1]{2,3,1,0:T(1,128)S(1)} %bitcast.188, f32[8,8,128,256]{3,2,1,0:T(8,128)} %exponential_multiply_fusion), kind=kOutput, calls=%fused_computation.38 | convolution fusion | flops 25165824 | bytes 8429568 | tf_op jit(solution)/shard_map/bkrc,bkc->br/dot_general | solution.py:87
  153.4 7.2 %fusion.14 = f32[8,1,8,128]{3,1,2,0:T(1,128)S(1)} fusion(f32[8,8,128,256]{3,2,1,0:T(8,128)S(1)} %copy-done.1, f32[8,256,1,1]{1,0,2,3:T(8,128)S(1)} %fusion.45), kind=kOutput, calls=%fused_computation.36 | convolution fusion | flops 25165824 | bytes 8429568 | tf_op jit(solution)/shard_map/bkrc,br->bkc/dot_general | solution.py:89
  161.4 3.7 all-to-all-start.2
  165.8 41.0 %psum.7 = f32[]{:T(128)} all-reduce(f32[]{:T(128)} %reduce_sum.58), channel_id=1, replica_groups=mesh['rows'=8,'cents'=4] {'rows','cents'}, use_global_device_ids=true, to_apply=%region_6.7 | all-reduce | flops 1 | bytes 8 | tf_op jit(solution)/shard_map/psum | solution.py:67
  210.3 12.0 %all_to_all.57 = f32[8,2,128]{2,1,0:T(2,128)S(1)} all-to-all(f32[8,2,128]{2,1,0:T(2,128)S(1)} %bitcast.192), channel_id=1, replica_groups=mesh['rows'=8,'cents'=4] {'rows'}, dimensions={0} | all-to-all | bytes 16384 | tf_op jit(solution)/shard_map/all_to_all | solution.py:97
  222.9 6.7 %fusion.12 = f32[8,1,256,1]{2,1,3,0:T(1,128)S(1)} fusion(f32[8,8,128,1]{2,3,1,0:T(1,128)S(1)} %bitcast.186, f32[8,8,128,256]{3,2,1,0:T(8,128)} %exponential_multiply_fusion), kind=kOutput, calls=%fused_computation.34 | convolution fusion | flops 25165824 | bytes 8429568 | tf_op jit(solution)/shard_map/bkrc,bkc->br/dot_general | solution.py:87
  229.6 9.4 %fusion.10 = f32[8,1,8,128]{3,1,2,0:T(1,128)S(1)} fusion(f32[8,8,128,256]{3,2,1,0:T(8,128)} %exponential_multiply_fusion, f32[8,256,1,1]{1,0,2,3:T(8,128)S(1)} %fusion.44), kind=kOutput, calls=%fused_computation.32 | convolution fusion | flops 25165824 | bytes 8429568 | tf_op jit(solution)/shard_map/bkrc,br->bkc/dot_general | solution.py:89
  239.3 8.9 %all_to_all.58 = f32[8,2,128]{2,1,0:T(2,128)S(1)} all-to-all(f32[8,2,128]{2,1,0:T(2,128)S(1)} %copy.26), channel_id=1, replica_groups=mesh['rows'=8,'cents'=4] {'rows'}, dimensions={0} | all-to-all | bytes 16384 | tf_op jit(solution)/shard_map/all_to_all | solution.py:94
  249.4 3.3 all-to-all-start.5
  252.9 6.4 %all-to-all-done.5 = f32[8,2,128]{2,1,0:T(2,128)S(1)} async-done(((f32[8,2,128]{2,1,0:T(2,128)}), f32[8,2,128]{2,1,0:T(2,128)S(1)}, u32[]{:S(2)}, u32[]{:S(2)}) %all-to-all-start.5) | async-done | bytes 8224 | tf_op jit(solution)/shard_map/all_to_all | solution.py:97
  259.8 6.7 %fusion.8 = f32[8,1,256,1]{2,1,3,0:T(1,128)S(1)} fusion(f32[8,8,128,1]{2,3,1,0:T(1,128)S(1)} %bitcast.187, f32[8,8,128,256]{3,2,1,0:T(8,128)} %exponential_multiply_fusion), kind=kOutput, calls=%fused_computation.30 | convolution fusion | flops 25165824 | bytes 8429568 | tf_op jit(solution)/shard_map/bkrc,bkc->br/dot_general | solution.py:87
  266.6 9.4 %fusion.6 = f32[8,1,8,128]{3,1,2,0:T(1,128)S(1)} fusion(f32[8,8,128,256]{3,2,1,0:T(8,128)} %exponential_multiply_fusion, f32[8,256,1,1]{1,0,2,3:T(8,128)S(1)} %fusion.43), kind=kOutput, calls=%fused_computation.28 | convolution fusion | flops 25165824 | bytes 8429568 | tf_op jit(solution)/shard_map/bkrc,br->bkc/dot_general | solution.py:89
  276.8 3.3 all-to-all-start.6
  280.2 6.4 %all-to-all-done.6 = f32[8,2,128]{2,1,0:T(2,128)S(1)} async-done(((f32[8,2,128]{2,1,0:T(2,128)}), f32[8,2,128]{2,1,0:T(2,128)S(1)}, u32[]{:S(2)}, u32[]{:S(2)}) %all-to-all-start.6) | async-done | bytes 8224 | tf_op jit(solution)/shard_map/all_to_all | solution.py:94
  287.9 3.5 all-to-all-start.7
  291.7 6.1 all-to-all-done.7
  298.4 6.7 %fusion.4 = f32[8,1,256,1]{2,1,3,0:T(1,128)S(1)} fusion(f32[8,8,128,1]{2,3,1,0:T(1,128)S(1)} %bitcast.184, f32[8,8,128,256]{3,2,1,0:T(8,128)} %exponential_multiply_fusion), kind=kOutput, calls=%fused_computation.26 | convolution fusion | flops 25165824 | bytes 8429568 | tf_op jit(solution)/shard_map/bkrc,bkc->br/dot_general | solution.py:101
  305.2 4.9 fusion.19
  310.1 3.2 fusion.32
  313.2 2.7 fusion.31
  315.9 2.7 fusion.30
  321.3 2.7 fusion.28
  324.0 2.7 fusion.27
  330.2 3.5 all-to-all-start.9
  333.8 5.1 fusion.25
  338.9 4.5 broadcast_in_dim.21
  343.4 8.7 %scatter_fusion = f32[16,128,1024]{2,1,0:T(8,128)} fusion(f32[16,128,1024]{2,1,0:T(8,128)} %broadcast_in_dim.21, s32[8]{0:T(128)S(1)} %get-tuple-element.9, f32[8,128,1024]{2,1,0:T(8,128)} %fusion.32), kind=kCustom, calls=%fused_computation.9 | custom fusion | flops 1048576 | bytes 12582944 | tf_op jit(solution)/shard_map/scatter-add | solution.py:117
  352.1 8.7 %scatter_fusion.1 = f32[16,128,1024]{2,1,0:T(8,128)} fusion(f32[16,128,1024]{2,1,0:T(8,128)} %scatter_fusion, s32[8]{0:T(128)S(1)} %get-tuple-element.8, f32[8,128,1024]{2,1,0:T(8,128)} %fusion.31), kind=kCustom, calls=%fused_computation.10 | custom fusion | flops 1048576 | bytes 12582944 | tf_op jit(solution)/shard_map/scatter-add | solution.py:117
  360.8 8.7 %scatter_fusion.2 = f32[16,128,1024]{2,1,0:T(8,128)} fusion(f32[16,128,1024]{2,1,0:T(8,128)} %scatter_fusion.1, s32[8]{0:T(128)S(1)} %get-tuple-element.7, f32[8,128,1024]{2,1,0:T(8,128)} %fusion.30), kind=kCustom, calls=%fused_computation.11 | custom fusion | flops 1048576 | bytes 12582944 | tf_op jit(solution)/shard_map/scatter-add | solution.py:117
  369.5 8.7 %scatter_fusion.3 = f32[16,128,1024]{2,1,0:T(8,128)} fusion(f32[16,128,1024]{2,1,0:T(8,128)} %scatter_fusion.2, s32[8]{0:T(128)S(1)} %get-tuple-element.6, f32[8,128,1024]{2,1,0:T(8,128)} %fusion.29), kind=kCustom, calls=%fused_computation.12 | custom fusion | flops 1048576 | bytes 12582944 | tf_op jit(solution)/shard_map/scatter-add | solution.py:117
  378.3 8.9 %scatter_fusion.4 = f32[16,128,1024]{2,1,0:T(8,128)} fusion(f32[16,128,1024]{2,1,0:T(8,128)} %scatter_fusion.3, s32[8]{0:T(128)S(1)} %get-tuple-element.5, f32[8,128,1024]{2,1,0:T(8,128)} %fusion.28), kind=kCustom, calls=%fused_computation.13 | custom fusion | flops 1048576 | bytes 12582944 | tf_op jit(solution)/shard_map/scatter-add | solution.py:117
  387.1 8.7 %scatter_fusion.5 = f32[16,128,1024]{2,1,0:T(8,128)} fusion(f32[16,128,1024]{2,1,0:T(8,128)} %scatter_fusion.4, s32[8]{0:T(128)S(1)} %get-tuple-element.4, f32[8,128,1024]{2,1,0:T(8,128)} %fusion.27), kind=kCustom, calls=%fused_computation.14 | custom fusion | flops 1048576 | bytes 12582944 | tf_op jit(solution)/shard_map/scatter-add | solution.py:117
  395.8 8.7 %scatter_fusion.6 = f32[16,128,1024]{2,1,0:T(8,128)} fusion(f32[16,128,1024]{2,1,0:T(8,128)} %scatter_fusion.5, s32[8]{0:T(128)S(1)} %get-tuple-element.3, f32[8,128,1024]{2,1,0:T(8,128)} %fusion.26), kind=kCustom, calls=%fused_computation.15 | custom fusion | flops 1048576 | bytes 12582944 | tf_op jit(solution)/shard_map/scatter-add | solution.py:117
  404.6 8.7 %scatter_fusion.7 = f32[16,128,1024]{2,1,0:T(8,128)} fusion(f32[16,128,1024]{2,1,0:T(8,128)} %scatter_fusion.6, s32[8]{0:T(128)S(1)} %get-tuple-element.2, f32[8,128,1024]{2,1,0:T(8,128)} %fusion.25), kind=kCustom, calls=%fused_computation.16 | custom fusion | flops 1048576 | bytes 12582944 | tf_op jit(solution)/shard_map/scatter-add | solution.py:117
  413.3 6.4 %all-to-all-start.8 = ((f32[8,2,128,1024]{3,2,1,0:T(8,128)}), f32[8,2,128,1024]{3,2,1,0:T(8,128)}, u32[]{:S(2)}, u32[]{:S(2)}) async-start(f32[8,2,128,1024]{3,2,1,0:T(8,128)} %bitcast.176), calls=%async_computation.8 | async-start | bytes 16777216 | tf_op jit(solution)/shard_map/all_to_all | solution.py:119
  420.4 174.5 %all-to-all-done.8 = f32[8,2,128,1024]{3,2,1,0:T(8,128)} async-done(((f32[8,2,128,1024]{3,2,1,0:T(8,128)}), f32[8,2,128,1024]{3,2,1,0:T(8,128)}, u32[]{:S(2)}, u32[]{:S(2)}) %all-to-all-start.8) | async-done | bytes 8388640 | tf_op jit(solution)/shard_map/all_to_all | solution.py:119
  594.8 8.2 %copy.44 = f32[2,8,128,1024]{3,1,2,0:T(8,128)S(1)} copy(f32[2,8,128,1024]{3,2,1,0:T(8,128)} %bitcast.82) | data formatting | bytes 16777216
  603.1 6.2 %fusion.49 = f32[16,131072]{1,0:T(8,128)} fusion(f32[16,131072]{1,0:T(8,128)S(1)} %bitcast.177, s32[16]{0:T(128)S(1)} %eq.106), kind=kOutput, calls=%fused_computation.102 | convolution fusion | flops 402653440 | bytes 16777280 | tf_op jit(solution)/shard_map/dot_general | solution.py:128
  609.3 6.3 %reshape.468 = f32[2048,1024]{1,0:T(8,128)} reshape(f32[16,131072]{1,0:T(8,128)} %fusion.49) | data formatting | bytes 16777216 | tf_op jit(solution)/shard_map/reshape | solution.py:132
  (76 shorter events, 22.7 us)
Async XLA Ops:
  3.4 13.6 %all-to-all-start = ((s32[8,1,2]{2,1,0:T(1,128)}), s32[8,1,2]{2,1,0:T(1,128)S(1)}, u32[]{:S(2)}, u32[]{:S(2)}) async-start(s32[8,1,2]{2,1,0:T(1,128)} %bitcast.2), calls=%async_computation | async-start | bytes 8192 | tf_op jit(solution)/shard_map/all_to_all | solution.py:72
  10.7 3.4 copy-start.3
  22.2 6.2 %copy-start.5 = (s32[8,8]{1,0:T(8,128)S(1)}, s32[8,8]{1,0:T(8,128)}, u32[]{:S(2)}) copy-start(s32[8,8]{1,0:T(8,128)} %param.8) | copy-start | bytes 772
  22.2 6.3 %copy-start.6 = (f32[2048]{0:T(1024)S(1)}, f32[2048]{0:T(1024)}, u32[]{:S(2)}) copy-start(f32[2048]{0:T(1024)} %param.7) | copy-start | bytes 24580
  22.2 6.3 %copy-start.7 = (s32[8]{0:T(128)S(1)}, s32[8]{0:T(128)}, u32[]{:S(2)}) copy-start(s32[8]{0:T(128)} %param.9) | copy-start | bytes 100
  22.3 98.8 %all-to-all-start.1 = ((bf16[8,2,128,1024]{3,2,1,0:T(8,128)(2,1)}), bf16[8,2,128,1024]{3,2,1,0:T(8,128)(2,1)}, u32[]{:S(2)}, u32[]{:S(2)}) async-start(bf16[8,2,128,1024]{3,2,1,0:T(8,128)(2,1)} %bitcast.180), calls=%async_computation.1 | async-start | bytes 8388608 | tf_op jit(solution)/shard_map/all_to_all | solution.py:74
  28.5 3.5 copy-start.4
  145.6 7.8 %copy-start.1 = (f32[8,8,128,256]{3,2,1,0:T(8,128)S(1)}, f32[8,8,128,256]{3,2,1,0:T(8,128)}, u32[]{:S(2)}) copy-start(f32[8,8,128,256]{3,2,1,0:T(8,128)} %exponential_multiply_fusion) | copy-start | bytes 25165828
  161.4 48.1 %all-to-all-start.2 = ((f32[8,2,128]{2,1,0:T(2,128)}), f32[8,2,128]{2,1,0:T(2,128)S(1)}, u32[]{:S(2)}, u32[]{:S(2)}) async-start(f32[8,2,128]{2,1,0:T(2,128)} %copy.25), calls=%async_computation.2 | async-start | bytes 16384 | tf_op jit(solution)/shard_map/all_to_all | solution.py:94
  249.4 9.8 %all-to-all-start.5 = ((f32[8,2,128]{2,1,0:T(2,128)}), f32[8,2,128]{2,1,0:T(2,128)S(1)}, u32[]{:S(2)}, u32[]{:S(2)}) async-start(f32[8,2,128]{2,1,0:T(2,128)} %bitcast.34), calls=%async_computation.5 | async-start | bytes 16384 | tf_op jit(solution)/shard_map/all_to_all | solution.py:97
  276.8 9.8 %all-to-all-start.6 = ((f32[8,2,128]{2,1,0:T(2,128)}), f32[8,2,128]{2,1,0:T(2,128)S(1)}, u32[]{:S(2)}, u32[]{:S(2)}) async-start(f32[8,2,128]{2,1,0:T(2,128)} %copy.27), calls=%async_computation.6 | async-start | bytes 16384 | tf_op jit(solution)/shard_map/all_to_all | solution.py:94
  287.9 10.0 %all-to-all-start.7 = ((f32[8,2,128]{2,1,0:T(2,128)}), f32[8,2,128]{2,1,0:T(2,128)S(1)}, u32[]{:S(2)}, u32[]{:S(2)}) async-start(f32[8,2,128]{2,1,0:T(2,128)} %bitcast.46), calls=%async_computation.7 | async-start | bytes 16384 | tf_op jit(solution)/shard_map/all_to_all | solution.py:97
  305.2 4.9 copy-start
  310.1 16.7 %copy-start.2 = (bf16[8,8,256,128]{2,3,1,0:T(8,128)(2,1)}, bf16[8,8,256,128]{2,3,1,0:T(8,128)(2,1)S(1)}, u32[]{:S(2)}) copy-start(bf16[8,8,256,128]{2,3,1,0:T(8,128)(2,1)S(1)} %get-tuple-element.11) | copy-start | bytes 12582916
  330.2 83.0 %all-to-all-start.9 = ((f32[8,2,128]{2,1,0:T(2,128)}), f32[8,2,128]{2,1,0:T(2,128)S(1)}, u32[]{:S(2)}, u32[]{:S(2)}) async-start(f32[8,2,128]{2,1,0:T(2,128)} %copy.28), calls=%async_computation.9 | async-start | bytes 16384 | tf_op jit(solution)/shard_map/all_to_all | solution.py:126
  413.3 181.6 %all-to-all-start.8 = ((f32[8,2,128,1024]{3,2,1,0:T(8,128)}), f32[8,2,128,1024]{3,2,1,0:T(8,128)}, u32[]{:S(2)}, u32[]{:S(2)}) async-start(f32[8,2,128,1024]{3,2,1,0:T(8,128)} %bitcast.176), calls=%async_computation.8 | async-start | bytes 16777216 | tf_op jit(solution)/shard_map/all_to_all | solution.py:119
where the time goes:
time: 620 us; the launch traced here: 616 us
  waiting for transfers between devices  280 us (45%)
  matrix products  102 us (16%)
  other arithmetic  89 us (14%)
  blocking collectives  61.9 us (10%)
  local copies, waits for them, and re-layouts  43.6 us (7%)
  starting transfers between devices  37.2 us (6%)
    all_to_all x1, waiting for transfers between devices, body(): lax.all_to_all(gathered_sums.reshape(rows_count, use_count, CB, D), 'rows...  174 us
    all_to_all x1, waiting for transfers between devices, body(): lax.all_to_all(lists_norm[local_in], 'rows', split_axis=0, concat_axis=0,...  86.4 us
    scatter-add x8, other arithmetic, body(): gathered_sums = gathered_sums.at[slot_target[:, slot_number]].add(slot_part)  69.9 us
    psum x1, blocking collectives, body(): weight_sum = lax.psum(jnp.sum(row_weight), ('rows', 'cents'))  41 us
    dot_general x4, matrix products, body(): row_sums = jnp.einsum('bkrc,bkc->br', kernel, picked, precision=HIGHEST)  27.9 us
    dot_general x3, matrix products, body(): jnp.einsum('bkrc,br->bkc', kernel, row_scale, precision=HIGHEST)  26 us
    dot_general x8, matrix products, body(): jnp.einsum('brc,brd->bcd', transport_half[:, slot_number], rows_norm, pre...  24.5 us
    dot_general x1, matrix products, body(): jnp.einsum('brd,bkcd->bkrc', rows_norm, picked_lists, preferred_element_t...  15.1 us
  transfers between devices with their start and end apart: 8, of which 6 were waited for; matrix products, arithmetic and copies ran while one was open for 15% of the time, Pallas kernels for 0%

commit v1 on v0

v1 whole, which is shorter than its diff:
```python
import functools

import jax
import jax.numpy as jnp
from jax import lax
from jax.experimental import pallas as pl
from jax.experimental.pallas import tpu as pltpu
from jax.sharding import PartitionSpec as P

D = 1024
RB = 256
CB = 128
USE = 2
ITERS = 3
BETA = 32.0
EPSILON = 1e-06
PRIOR = 0.25
HIGHEST = lax.Precision.HIGHEST
MESH = pl.DeviceIdType.MESH
F32 = jnp.float32
BF16 = jnp.bfloat16


def normalize(values):
    widened = values.astype(F32)
    factor = lax.rsqrt(jnp.mean(widened * widened, axis=-1, keepdims=True) + EPSILON)
    return (widened * factor).astype(BF16)


def flipped(index, offset):
    result = index
    bit = 1
    while bit <= offset:
        if offset & bit:
            result = result + bit * (1 - 2 * ((index // bit) % 2))
        bit *= 2
    return result


def peer_order(rows_count):
    half = rows_count // 2
    quarter = max(half // 2, 1)
    far = list(range(half + quarter, rows_count)) + list(range(half, half + quarter))
    near = sorted(range(1, half), key=lambda j: -j)
    return [j for j in far if j > 0] + near


def main_kernel(
    rows_count, cents_count, list_total,
    groups, centroids, weights, id_message, id_column, use_table, live_table,
    sums_out, mass_out, ids_out, target_out,
    rows, lists, send, lists_in, kernel, left, weight_column, row_scale,
    ids_scalar, parts, parts_in, scales, match, mass_send, weight_send, weight_in, total,
    load_sem, ids_send_sem, ids_recv_sem, list_send_sem, list_recv_sem, part_send_sem, part_recv_sem,
    sum_send_sem, sum_recv_sem, mass_send_sem, mass_recv_sem, weight_send_sem, weight_recv_sem,
):
    me = lax.axis_index("rows")
    cent = lax.axis_index("cents")
    distinct = rows_count * USE
    list_blocks = lists.shape[0]
    row_blocks = rows.shape[0] // RB
    order = peer_order(rows_count)
    peers = {j: (flipped(me, j), cent) for j in order}
    cent_peers = {q: (me, (cent + q) % cents_count) for q in range(1, cents_count)}

    load_lists = pltpu.make_async_copy(centroids, lists, load_sem.at[0])
    load_lists.start()
    load_rows = pltpu.make_async_copy(groups, rows, load_sem.at[1])
    load_rows.start()

    barrier = pltpu.get_barrier_semaphore()
    for peer in list(peers.values()) + list(cent_peers.values()):
        pl.semaphore_signal(barrier, inc=1, device_id=peer, device_id_type=MESH)
    pl.semaphore_wait(barrier, len(peers) + len(cent_peers))

    def remote(source, target, send_sem, recv_sem, peer):
        copy = pltpu.make_async_remote_copy(
            src_ref=source, dst_ref=target, send_sem=send_sem, recv_sem=recv_sem,
            device_id=peer, device_id_type=MESH,
        )
        copy.start()
        return copy

    id_copies = [
        remote(id_message, ids_out.at[j], ids_send_sem.at[j], ids_recv_sem.at[j], peers[j])
        for j in order
    ]
    ids_out[0] = id_message[...]
    weight_send[...] = jnp.broadcast_to(jnp.sum(weights[...], keepdims=True), weight_send.shape)
    weight_copies = [
        remote(weight_send, weight_in.at[q], weight_send_sem.at[q], weight_recv_sem.at[q], cent_peers[q])
        for q in cent_peers
    ]
    for copy in id_copies:
        copy.wait_recv()
    to_scalar = pltpu.make_async_copy(ids_out, ids_scalar, load_sem.at[2])
    to_scalar.start()
    to_scalar.wait()
    load_lists.wait()

    def normalized_list(j, use):
        wanted = lax.rem(ids_scalar[j, 0, USE * j + use], list_blocks)
        return normalize(lists[wanted])

    list_copies = {}
    for j in order:
        for use in range(USE):
            send[j, use * CB : (use + 1) * CB, :] = normalized_list(j, use)
        list_copies[j] = remote(
            send.at[j], lists_in.at[j], list_send_sem.at[j], list_recv_sem.at[j], peers[j]
        )
    own_ids = [lax.rem(ids_scalar[0, 0, use], list_blocks) for use in range(USE)]
    for use in range(USE):
        lists_in[0, use * CB : (use + 1) * CB, :] = normalize(lists[own_ids[use]])

    load_rows.wait()

    def normalize_rows(index, carry):
        where = pl.ds(pl.multiple_of(index * CB, CB), CB)
        rows[where, :] = normalize(rows[where, :])
        return carry

    lax.fori_loop(0, row_blocks * RB // CB, normalize_rows, 0)

    for index in range(weights.shape[0]):
        spread = jnp.broadcast_to(weights[index : index + 1, :], (128, 128))
        weight_column[index * 128 : (index + 1) * 128, :] = spread.T

    wide = match.shape[1]
    lane = lax.broadcasted_iota(jnp.int32, (1, wide), 1)
    id_row = jnp.zeros((1, wide), jnp.int32)
    for j in range(rows_count):
        id_row = id_row + jnp.where(lane // distinct == j, ids_out[j, 0:1, :], 0)
    match[...] = (id_column[...] == id_row).astype(F32)

    for copy in weight_copies:
        copy.wait_recv()
    group_weight = weight_send[...]
    for q in cent_peers:
        group_weight = group_weight + weight_in[q]
    scales[...] = jnp.ones_like(scales)
    parts[...] = jnp.zeros_like(parts)
    parts[0, distinct : distinct + 8, :] = group_weight

    def scores_of(j):
        def one(block, carry):
            where = pl.ds(pl.multiple_of(block * RB, RB), RB)
            both = lax.dot_general(
                rows[where, :], lists_in[j], (((1,), (1,)), ((), ())), preferred_element_type=F32
            )
            use = use_table[block, j : j + 1, :CB]
            picked = jnp.where(use > 0.5, both[:, CB:], both[:, :CB])
            kernel[block, j] = jnp.exp(picked * (BETA / D)) * live_table[block, j : j + 1, :]
            return carry

        lax.fori_loop(0, row_blocks, one, 0)

    scores_of(0)
    for j in order[::-1]:
        list_copies[j].wait_recv()
        scores_of(j)

    def scale_of(block, j):
        use = use_table[block, j : j + 1, :CB]
        return jnp.where(use > 0.5, scales[USE * j + 1 : USE * j + 2, :], scales[USE * j : USE * j + 1, :])

    def row_step(block):
        total_row = jnp.zeros((RB, CB), F32)
        for j in range(rows_count):
            total_row = total_row + kernel[block, j] * scale_of(block, j)
        where = pl.ds(pl.multiple_of(block * RB, RB), RB)
        return weight_column[where, :] / jnp.sum(total_row, axis=1, keepdims=True)

    part_copies = []
    for step in range(ITERS):
        def column_step(block, carry):
            factor = row_step(block)
            for j in range(rows_count):
                column = jnp.sum(kernel[block, j] * factor, axis=0, keepdims=True)
                use = use_table[block, j : j + 1, :CB]
                low, high = USE * j, USE * j + 1
                parts[step, low : low + 1, :] += column * (1.0 - use)
                parts[step, high : high + 1, :] += column * use
            return carry

        lax.fori_loop(0, row_blocks, column_step, 0)
        copies = [
            remote(
                parts.at[step], parts_in.at[step, j],
                part_send_sem.at[step, j], part_recv_sem.at[step, j], peers[j],
            )
            for j in order
        ]
        parts_in[step, 0] = parts[step]
        for copy in copies:
            copy.wait_recv()
        part_copies += copies
        if step == 0:
            mass = parts_in[0, 0, distinct : distinct + 8, :]
            for j in range(1, rows_count):
                mass = mass + parts_in[0, j, distinct : distinct + 8, :]
            total[...] = mass / list_total
        column_all = jnp.dot(
            match[...],
            parts_in[step, :, :distinct, :].reshape(rows_count * distinct, CB),
            precision=HIGHEST, preferred_element_type=F32,
        )
        target = total[0:1, :]
        scales[...] = target / (column_all + PRIOR * target)

    def last_rows(block, carry):
        where = pl.ds(pl.multiple_of(block * RB, RB), RB)
        row_scale[where, :] = row_step(block)
        return carry

    lax.fori_loop(0, row_blocks, last_rows, 0)
    target_out[...] = total[...]

    sum_copies = []
    mass_copies = []
    keep = []
    for j in order + [0]:
        if j:
            list_copies[j].wait_send()
        mass_send[j] = jnp.zeros((8, CB), F32)

        def transport_of(block, carry):
            where = pl.ds(pl.multiple_of(block * RB, RB), RB)
            transport = row_scale[where, :] * kernel[block, j] * scale_of(block, j)
            column = jnp.sum(transport, axis=0, keepdims=True)
            use = use_table[block, j : j + 1, :]
            mass_send[j, 0:1, :] += column * (1.0 - use[:, :CB])
            mass_send[j, 1:2, :] += column * use[:, :CB]
            turned = transport.T
            left[:CB, where] = jnp.where(use > 0.5, 0.0, turned).astype(BF16)
            left[CB:, where] = jnp.where(use > 0.5, turned, 0.0).astype(BF16)
            return carry

        lax.fori_loop(0, row_blocks, transport_of, 0)

        def product(chunk, carry):
            where = pl.ds(pl.multiple_of(chunk * 256, 256), 256)
            send[j, :, where] = jnp.dot(
                left[...], rows[:, where], preferred_element_type=F32
            ).astype(BF16)
            return carry

        lax.fori_loop(0, D // 256, product, 0)
        if j:
            sum_copies.append(
                remote(send.at[j], sums_out.at[j], sum_send_sem.at[j], sum_recv_sem.at[j], peers[j])
            )
            mass_copies.append(
                remote(
                    mass_send.at[j], mass_out.at[j], mass_send_sem.at[j], mass_recv_sem.at[j], peers[j]
                )
            )
        else:
            mass_out[0] = mass_send[0]
            own = pltpu.make_async_copy(send.at[0], sums_out.at[0], load_sem.at[0])
            own.start()
            keep.append(own)

    for copy in id_copies + weight_copies + part_copies:
        copy.wait_send()
    for copy in mass_copies + sum_copies:
        copy.wait()
    for copy in keep:
        copy.wait()


def combine_kernel(ids, sums, mass, target, out, load):
    block = pl.program_id(0)
    rows_count = sums.shape[0]
    list_blocks = load.shape[0]
    out[...] = jnp.zeros_like(out)
    total = jnp.zeros((1, CB), F32)
    for j in range(rows_count):
        for use in range(USE):
            hit = lax.rem(ids[j, 0, USE * j + use], list_blocks) == block

            @pl.when(hit)
            def _():
                out[...] += sums[j, use * CB : (use + 1) * CB, :].astype(F32)

            total = total + jnp.where(hit, mass[j, use : use + 1, :], 0.0)
    load[pl.ds(block, 1), :] = total / target[0:1, :]


def routing(block_ids, block_counts, list_blocks, rows_count, cents_count):
    holder = block_ids // list_blocks // cents_count
    local = block_ids % list_blocks
    offsets = lax.axis_index("rows") ^ jnp.arange(rows_count, dtype=jnp.int32)
    hit = holder[:, :, None] == offsets[None, None, :]
    slot = jnp.arange(block_ids.shape[1], dtype=jnp.int32)
    alive = slot[None, :] < block_counts[:, None]
    named = jnp.sum(jnp.where(hit, local[:, :, None], 0), axis=1)
    present = jnp.any(hit, axis=1)
    live = jnp.any(hit & alive[:, :, None], axis=1)
    low = jnp.min(jnp.where(present, named, list_blocks), axis=0)
    high = jnp.max(jnp.where(present, named, -1), axis=0)
    use = named == high[None, :]
    ids = offsets[:, None] * list_blocks + jnp.stack([low, high], axis=1)
    return use, live, ids.reshape(-1)


def body(groups, centroids, row_weight, block_ids, block_counts):
    rows_count = lax.axis_size("rows")
    cents_count = lax.axis_size("cents")
    row_blocks = block_ids.shape[0]
    list_blocks = centroids.shape[0] // CB
    list_total = list_blocks * CB * rows_count * cents_count
    distinct = rows_count * USE
    wide = rows_count * distinct
    use, live, ids = routing(block_ids, block_counts, list_blocks, rows_count, cents_count)
    id_message = jnp.broadcast_to(jnp.tile(ids, rows_count)[None, :], (8, wide))
    id_column = jnp.broadcast_to(ids[:, None], (distinct, wide))
    use_table = jnp.broadcast_to(use.astype(F32)[:, :, None], (row_blocks, rows_count, RB))
    live_table = jnp.broadcast_to(live.astype(F32)[:, :, None], (row_blocks, rows_count, CB))
    any_space = pl.BlockSpec(memory_space=pl.ANY)
    vmem = pl.BlockSpec(memory_space=pltpu.VMEM)
    dma = pltpu.SemaphoreType.DMA
    row_total = row_blocks * RB
    sums, mass, all_ids, target = pl.pallas_call(
        functools.partial(main_kernel, rows_count, cents_count, list_total),
        out_shape=(
            jax.ShapeDtypeStruct((rows_count, USE * CB, D), BF16),
            jax.ShapeDtypeStruct((rows_count, 8, CB), F32),
            jax.ShapeDtypeStruct((rows_count, 8, wide), jnp.int32),
            jax.ShapeDtypeStruct((8, CB), F32),
        ),
        in_specs=[any_space, any_space, vmem, vmem, vmem, vmem, vmem],
        out_specs=(any_space, vmem, vmem, vmem),
        scratch_shapes=[
            pltpu.VMEM((row_total, D), BF16),
            pltpu.VMEM((list_blocks, CB, D), BF16),
            pltpu.VMEM((rows_count, USE * CB, D), BF16),
            pltpu.VMEM((rows_count, USE * CB, D), BF16),
            pltpu.VMEM((row_blocks, rows_count, RB, CB), F32),
            pltpu.VMEM((USE * CB, row_total), BF16),
            pltpu.VMEM((row_total, CB), F32),
            pltpu.VMEM((row_total, CB), F32),
            pltpu.SMEM((rows_count, 8, wide), jnp.int32),
            pltpu.VMEM((ITERS, distinct + 8, CB), F32),
            pltpu.VMEM((ITERS, rows_count, distinct + 8, CB), F32),
            pltpu.VMEM((distinct, CB), F32),
            pltpu.VMEM((distinct, wide), F32),
            pltpu.VMEM((rows_count, 8, CB), F32),
            pltpu.VMEM((8, CB), F32),
            pltpu.VMEM((cents_count, 8, CB), F32),
            pltpu.VMEM((8, CB), F32),
            dma((3,)),
            dma((rows_count,)), dma((rows_count,)),
            dma((rows_count,)), dma((rows_count,)),
            dma((ITERS, rows_count)), dma((ITERS, rows_count)),
            dma((rows_count,)), dma((rows_count,)),
            dma((rows_count,)), dma((rows_count,)),
            dma((cents_count,)), dma((cents_count,)),
        ],
        compiler_params=pltpu.CompilerParams(
            collective_id=0, has_side_effects=True, vmem_limit_bytes=56 * 2**20
        ),
        cost_estimate=pl.CostEstimate(
            flops=8 * row_total * D * distinct * CB // 2, bytes_accessed=16 * 2**20, transcendentals=0
        ),
        name="assign",
    )(groups, centroids.reshape(list_blocks, CB, D), row_weight.reshape(-1, 128),
      id_message, id_column, use_table, live_table)
    out, load = pl.pallas_call(
        combine_kernel,
        grid=(list_blocks,),
        out_shape=(
            jax.ShapeDtypeStruct((list_blocks * CB, D), F32),
            jax.ShapeDtypeStruct((list_blocks, CB), F32),
        ),
        in_specs=[
            pl.BlockSpec(memory_space=pltpu.SMEM),
            pl.BlockSpec((rows_count, USE * CB, D), lambda block: (0, 0, 0)),
            pl.BlockSpec((rows_count, 8, CB), lambda block: (0, 0, 0)),
            pl.BlockSpec((8, CB), lambda block: (0, 0)),
        ],
        out_specs=(
            pl.BlockSpec((CB, D), lambda block: (block, 0)),
            pl.BlockSpec((list_blocks, CB), lambda block: (0, 0)),
        ),
        compiler_params=pltpu.CompilerParams(
            dimension_semantics=("arbitrary",), vmem_limit_bytes=48 * 2**20
        ),
        name="combine",
    )(all_ids, sums, mass, target)
    return out, load.reshape(-1)


def solution(mesh):
    placed = (
        P(("rows", "cents"), None),
        P(("rows", "cents"), None),
        P(("rows", "cents")),
        P(("rows", "cents"), None),
        P(("rows", "cents")),
    )
    return jax.shard_map(
        body,
        mesh=mesh,
        in_specs=placed,
        out_specs=(P(("rows", "cents"), None), P(("rows", "cents"))),
        check_vma=False,
    )
```

time: 620 us -> 251 us (0.40)
  waiting for transfers between devices: 280 us -> 0 us
  Pallas kernels: 0 us -> 240 us
  matrix products: 102 us -> 0 us
  other arithmetic: 89 us -> 1.67 us
  blocking collectives: 61.9 us -> 0 us
  starting transfers between devices: 37.2 us -> 0 us
  local copies, waits for them, and re-layouts: 43.6 us -> 7.27 us
    all_to_all x8 -> x0, waiting for transfers between devices: 280 us -> none  [the longest x1 174 us: body(): lax.all_to_all(gathered_sums.reshape(rows_count, use_count, CB, D), 'rows...]
    pallas_call x0 -> x2, Pallas kernels: none -> 240 us  [the longest x1 231 us: body(): pl.pallas_call(functools.partial(main_kernel, rows_count, cents_count, li...]
    dot_general x25 -> x0, matrix products: 102 us -> none  [the longest x4 27.9 us: body(): row_sums = jnp.einsum('bkrc,bkc->br', kernel, picked, precision=HIGHEST)]
    scatter-add x8 -> x0, other arithmetic: 69.9 us -> none  [body(): gathered_sums = gathered_sums.at[slot_target[:, slot_number]].add(slot_part)]
    psum x1 -> x0, blocking collectives: 41 us -> none  [body(): weight_sum = lax.psum(jnp.sum(row_weight), ('rows', 'cents'))]
    all_to_all x8 -> x0, starting transfers between devices: 37.2 us -> none  [the longest x1 7.25 us: body(): lax.all_to_all(request_table, 'rows', split_axis=0, concat_axis=0, tiled=...]
    all_to_all x2 -> x0, blocking collectives: 20.9 us -> none  [the longest x1 12 us: body(): lax.all_to_all(scales[local_in], 'rows', split_axis=0, concat_axis=0, til...]
    gather x10 -> x0, local copies, waits for them, and re-layouts: 19.9 us -> none  [the longest x1 9.4 us: body(): arrived.reshape(-1, CB, D)[distinct_of_pair]]
  transfers between devices with their start and end apart: 8 -> 0, of which waited for: 6 -> 0; matrix products, arithmetic and copies ran while one was open for 15% -> 0% of each run, Pallas kernels for 0% -> 0%
where the time goes in v1:
time: 251 us; the launch traced here: 250 us
  Pallas kernels  240 us (96%)
  local copies, waits for them, and re-layouts  7.27 us (3%)
    pallas_call x1, Pallas kernels, body(): pl.pallas_call(functools.partial(main_kernel, rows_count, cents_count, li...  231 us
    pallas_call x1, Pallas kernels, body(): pl.pallas_call(combine_kernel, grid=(list_blocks,), out_shape=(jax.ShapeD...  9.82 us

profile of v1, /device:TPU:0, one launch (start us, length us, event | category | flops | bytes accessed | tf_op | source)
XLA Modules:
  0.0 250.1 jit_solution(17391931958414674495)
XLA Ops:
  0.6 0.7 iota_compare_fusion
  1.4 0.7 add_select_fusion
  2.1 0.1 fusion
  2.2 0.1 fusion.1
  2.3 0.1 copy.9
  2.4 0.1 add.30
  2.5 0.1 broadcast_in_dim.27
  2.6 0.6 broadcast_in_dim.28.id_message
  3.2 0.7 broadcast_in_dim.29.id_column
  3.9 0.7 broadcast_in_dim.31.live_table
  4.5 0.7 broadcast_in_dim.30.use_table
  5.2 230.7 %assign.1 = (bf16[8,256,1024]{2,1,0:T(8,128)(2,1)}, f32[8,8,128]{2,1,0:T(8,128)}, s32[8,8,128]{2,1,0:T(8,128)}, f32[8,128]{1,0:T(8,128)}) custom-call(bf16[2048,1024]{1,0:T(8,128)(2,1)} %groups.1, bf16[16,128,1024]{2,1,0:T(8,128)(2,1)} %bitcast.7, f32[16,128]{1,0:T(8,128)} %bitcast.8, s32[8,128]{1,0:T(8,128)} %broadcast_in_dim.28.id_message, ...), custom_call_target="tpu_custom_call" | custom-call | flops 17179869184 | bytes 16777216 | tf_op jit(solution)/shard_map/assign/pallas_call | solution.py:324
  235.9 0.0 copy-start
  235.9 2.2 copy-done
  238.1 0.0 copy-start.1
  238.1 0.8 copy-done.1
  238.9 0.0 copy-start.2
  238.9 0.8 copy-done.2
  239.6 0.0 copy-start.3
  239.6 0.7 copy-done.3
  240.3 9.8 %combine.1 = (f32[2048,1024]{1,0:T(8,128)}, f32[16,128]{1,0:T(8,128)}) custom-call(s32[8,8,128]{2,1,0:T(8,128)S(1)} %copy-done.2, bf16[8,256,1024]{2,1,0:T(8,128)(2,1)S(1)} %copy-done, f32[8,8,128]{2,1,0:T(8,128)S(1)} %copy-done.1, f32[8,128]{1,0:T(8,128)S(1)} %copy-done.3), custom_call_target="tpu_custom_call" | custom-call | tf_op jit(solution)/shard_map/combine/pallas_call | solution.py:369
  (6 shorter events, 0.0 us)
Async XLA Ops:
  235.9 2.2 copy-start
  238.1 0.8 copy-start.1
  238.9 0.8 copy-start.2
  239.6 0.7 copy-start.3

commit v2 on v1

--- a/solution.py
+++ b/solution.py
@@ -39,17 +39,17 @@
 
 def peer_order(rows_count):
     half = rows_count // 2
-    quarter = max(half // 2, 1)
+    quarter = half // 2
     far = list(range(half + quarter, rows_count)) + list(range(half, half + quarter))
-    near = sorted(range(1, half), key=lambda j: -j)
-    return [j for j in far if j > 0] + near
+    return far, list(range(half - 1, 0, -1))
 
 
 def main_kernel(
     rows_count, cents_count, list_total,
-    groups, centroids, weights, id_message, id_column, use_table, live_table,
-    sums_out, mass_out, ids_out, target_out,
+    groups, centroids, weights, block_ids, block_counts,
+    sums_out, mass_out, ids_out,
     rows, lists, send, lists_in, kernel, left, weight_column, row_scale,
+    id_message, id_column, use_table, live_table, column_parts,
     ids_scalar, parts, parts_in, scales, match, mass_send, weight_send, weight_in, total,
     load_sem, ids_send_sem, ids_recv_sem, list_send_sem, list_recv_sem, part_send_sem, part_recv_sem,
     sum_send_sem, sum_recv_sem, mass_send_sem, mass_recv_sem, weight_send_sem, weight_recv_sem,
@@ -59,7 +59,8 @@
     distinct = rows_count * USE
     list_blocks = lists.shape[0]
     row_blocks = rows.shape[0] // RB
-    order = peer_order(rows_count)
+    far, near = peer_order(rows_count)
+    order = far + near
     peers = {j: (flipped(me, j), cent) for j in order}
     cent_peers = {q: (me, (cent + q) % cents_count) for q in range(1, cents_count)}
 
@@ -71,6 +72,30 @@
     barrier = pltpu.get_barrier_semaphore()
     for peer in list(peers.values()) + list(cent_peers.values()):
         pl.semaphore_signal(barrier, inc=1, device_id=peer, device_id_type=MESH)
+
+    ids = block_ids[...]
+    slot = lax.broadcasted_iota(jnp.int32, ids.shape, 1)
+    alive = slot < block_counts[...]
+    place = lax.broadcasted_iota(jnp.int32, id_message.shape, 1) % distinct
+    message = jnp.zeros(id_message.shape, jnp.int32)
+    for j in range(rows_count):
+        base = (flipped(me, j) * cents_count + cent) * list_blocks
+        inside = (ids >= base) & (ids < base + list_blocks)
+        named = jnp.max(jnp.where(inside, ids - base, -1), axis=1, keepdims=True)
+        live = jnp.max(jnp.where(inside & alive, 1.0, 0.0), axis=1, keepdims=True)
+        low = jnp.min(jnp.where(named >= 0, named, list_blocks), axis=0, keepdims=True)
+        high = jnp.max(named, axis=0, keepdims=True)
+        uses = jnp.broadcast_to((named == high).astype(F32), (row_blocks, RB))
+        lives = jnp.broadcast_to(live, (row_blocks, CB))
+        for block in range(row_blocks):
+            use_table[block, j : j + 1, :] = uses[block : block + 1, :]
+            live_table[block, j : j + 1, :] = lives[block : block + 1, :]
+        for use, picked in enumerate((low, high)):
+            message = jnp.where(place == USE * j + use, base + picked, message)
+            row = USE * j + use
+            id_column[row : row + 1, :] = jnp.broadcast_to(base + picked, (1, id_column.shape[1]))
+    id_message[...] = message
+
     pl.semaphore_wait(barrier, len(peers) + len(cent_peers))
 
     def remote(source, target, send_sem, recv_sem, peer):
@@ -103,12 +128,17 @@
         return normalize(lists[wanted])
 
     list_copies = {}
-    for j in order:
-        for use in range(USE):
-            send[j, use * CB : (use + 1) * CB, :] = normalized_list(j, use)
+
+    def start_lists(j):
         list_copies[j] = remote(
             send.at[j], lists_in.at[j], list_send_sem.at[j], list_recv_sem.at[j], peers[j]
         )
+
+    for j in far[:1] + near + far[1:]:
+        for use in range(USE):
+            send[j, use * CB : (use + 1) * CB, :] = normalized_list(j, use)
+        if j in near or j == far[0]:
+            start_lists(j)
     own_ids = [lax.rem(ids_scalar[0, 0, use], list_blocks) for use in range(USE)]
     for use in range(USE):
         lists_in[0, use * CB : (use + 1) * CB, :] = normalize(lists[own_ids[use]])
@@ -153,10 +183,16 @@
             kernel[block, j] = jnp.exp(picked * (BETA / D)) * live_table[block, j : j + 1, :]
             return carry
 
-        lax.fori_loop(0, row_blocks, one, 0)
+        lax.fori_loop(0, row_blocks, one, 0, unroll=2)
 
     scores_of(0)
-    for j in order[::-1]:
+    for j in near:
+        list_copies[j].wait_recv()
+        scores_of(j)
+    for index, j in enumerate(far):
+        list_copies[j].wait_send()
+        if index + 1 < len(far):
+            start_lists(far[index + 1])
         list_copies[j].wait_recv()
         scores_of(j)
 
@@ -176,14 +212,15 @@
         def column_step(block, carry):
             factor = row_step(block)
             for j in range(rows_count):
-                column = jnp.sum(kernel[block, j] * factor, axis=0, keepdims=True)
+                column = jnp.sum((kernel[block, j] * factor).reshape(RB // 8, 8, CB), axis=0)
                 use = use_table[block, j : j + 1, :CB]
-                low, high = USE * j, USE * j + 1
-                parts[step, low : low + 1, :] += column * (1.0 - use)
-                parts[step, high : high + 1, :] += column * use
+                column_parts[USE * j] += column * (1.0 - use)
+                column_parts[USE * j + 1] += column * use
             return carry
 
-        lax.fori_loop(0, row_blocks, column_step, 0)
+        column_parts[...] = jnp.zeros_like(column_parts)
+        lax.fori_loop(0, row_blocks, column_step, 0, unroll=2)
+        parts[step, :distinct, :] = jnp.sum(column_parts[...], axis=1)
         copies = [
             remote(
                 parts.at[step], parts_in.at[step, j],
@@ -213,14 +250,13 @@
         row_scale[where, :] = row_step(block)
         return carry
 
-    lax.fori_loop(0, row_blocks, last_rows, 0)
-    target_out[...] = total[...]
+    lax.fori_loop(0, row_blocks, last_rows, 0, unroll=2)
 
     sum_copies = []
     mass_copies = []
     keep = []
     for j in order + [0]:
-        if j:
+        if j in near:
             list_copies[j].wait_send()
         mass_send[j] = jnp.zeros((8, CB), F32)
 
@@ -236,7 +272,8 @@
             left[CB:, where] = jnp.where(use > 0.5, turned, 0.0).astype(BF16)
             return carry
 
-        lax.fori_loop(0, row_blocks, transport_of, 0)
+        lax.fori_loop(0, row_blocks, transport_of, 0, unroll=2)
+        mass_send[j] = mass_send[j] / total[...]
 
         def product(chunk, carry):
             where = pl.ds(pl.multiple_of(chunk * 256, 256), 256)
@@ -269,39 +306,51 @@
         copy.wait()
 
 
-def combine_kernel(ids, sums, mass, target, out, load):
-    block = pl.program_id(0)
+def combine_kernel(
+    sums, mass, ids, out, load, sums_here, mass_here, ids_scalar, whole, in_sem, out_sem
+):
     rows_count = sums.shape[0]
     list_blocks = load.shape[0]
-    out[...] = jnp.zeros_like(out)
-    total = jnp.zeros((1, CB), F32)
-    for j in range(rows_count):
-        for use in range(USE):
-            hit = lax.rem(ids[j, 0, USE * j + use], list_blocks) == block
+    copies = [
+        pltpu.make_async_copy(ids, ids_scalar, in_sem.at[0]),
+        pltpu.make_async_copy(mass, mass_here, in_sem.at[1]),
+    ]
+    copies += [
+        pltpu.make_async_copy(sums.at[j], sums_here.at[j], in_sem.at[2 + j]) for j in range(rows_count)
+    ]
+    for copy in copies:
+        copy.start()
+
+    def clear(block, carry):
+        whole[block] = jnp.zeros(whole.shape[1:], F32)
+        return carry
+
+    lax.fori_loop(0, list_blocks, clear, 0)
+    for copy in copies:
+        copy.wait()
+    local = [
+        (j, use, lax.rem(ids_scalar[j, 0, USE * j + use], list_blocks))
+        for j in range(rows_count)
+        for use in range(USE)
+    ]
+
+    def one(block, carry):
+        total = jnp.zeros((1, CB), F32)
+        for j, use, named in local:
+            hit = named == block
 
             @pl.when(hit)
             def _():
-                out[...] += sums[j, use * CB : (use + 1) * CB, :].astype(F32)
-
-            total = total + jnp.where(hit, mass[j, use : use + 1, :], 0.0)
-    load[pl.ds(block, 1), :] = total / target[0:1, :]
-
-
-def routing(block_ids, block_counts, list_blocks, rows_count, cents_count):
-    holder = block_ids // list_blocks // cents_count
-    local = block_ids % list_blocks
-    offsets = lax.axis_index("rows") ^ jnp.arange(rows_count, dtype=jnp.int32)
-    hit = holder[:, :, None] == offsets[None, None, :]
-    slot = jnp.arange(block_ids.shape[1], dtype=jnp.int32)
-    alive = slot[None, :] < block_counts[:, None]
-    named = jnp.sum(jnp.where(hit, local[:, :, None], 0), axis=1)
-    present = jnp.any(hit, axis=1)
-    live = jnp.any(hit & alive[:, :, None], axis=1)
-    low = jnp.min(jnp.where(present, named, list_blocks), axis=0)
-    high = jnp.max(jnp.where(present, named, -1), axis=0)
-    use = named == high[None, :]
-    ids = offsets[:, None] * list_blocks + jnp.stack([low, high], axis=1)
-    return use, live, ids.reshape(-1)
+                whole[block] += sums_here[j, use * CB : (use + 1) * CB, :].astype(F32)
+
+            total = total + jnp.where(hit, mass_here[j, use : use + 1, :], 0.0)
+        load[pl.ds(block, 1), :] = total
+        pltpu.make_async_copy(whole.at[block], out.at[block], out_sem.at[block]).start()
+        return carry
+
+    lax.fori_loop(0, list_blocks, one, 0)
+    for block in range(list_blocks):
+        pltpu.make_async_copy(whole.at[block], out.at[block], out_sem.at[block]).wait()
 
 
 def body(groups, centroids, row_weight, block_ids, block_counts):
@@ -312,25 +361,20 @@
     list_total = list_blocks * CB * rows_count * cents_count
     distinct = rows_count * USE
     wide = rows_count * distinct
-    use, live, ids = routing(block_ids, block_counts, list_blocks, rows_count, cents_count)
-    id_message = jnp.broadcast_to(jnp.tile(ids, rows_count)[None, :], (8, wide))
-    id_column = jnp.broadcast_to(ids[:, None], (distinct, wide))
-    use_table = jnp.broadcast_to(use.astype(F32)[:, :, None], (row_blocks, rows_count, RB))
-    live_table = jnp.broadcast_to(live.astype(F32)[:, :, None], (row_blocks, rows_count, CB))
+    count_table = jnp.broadcast_to(block_counts[:, None], block_ids.shape)
     any_space = pl.BlockSpec(memory_space=pl.ANY)
     vmem = pl.BlockSpec(memory_space=pltpu.VMEM)
     dma = pltpu.SemaphoreType.DMA
     row_total = row_blocks * RB
-    sums, mass, all_ids, target = pl.pallas_call(
+    sums, mass, all_ids = pl.pallas_call(
         functools.partial(main_kernel, rows_count, cents_count, list_total),
         out_shape=(
             jax.ShapeDtypeStruct((rows_count, USE * CB, D), BF16),
             jax.ShapeDtypeStruct((rows_count, 8, CB), F32),
             jax.ShapeDtypeStruct((rows_count, 8, wide), jnp.int32),
-            jax.ShapeDtypeStruct((8, CB), F32),
         ),
-        in_specs=[any_space, any_space, vmem, vmem, vmem, vmem, vmem],
-        out_specs=(any_space, vmem, vmem, vmem),
+        in_specs=[any_space, any_space, vmem, vmem, vmem],
+        out_specs=(any_space, vmem, vmem),
         scratch_shapes=[
             pltpu.VMEM((row_total, D), BF16),
             pltpu.VMEM((list_blocks, CB, D), BF16),
@@ -340,6 +384,11 @@
             pltpu.VMEM((USE * CB, row_total), BF16),
             pltpu.VMEM((row_total, CB), F32),
             pltpu.VMEM((row_total, CB), F32),
+            pltpu.VMEM((8, wide), jnp.int32),
+            pltpu.VMEM((distinct, wide), jnp.int32),
+            pltpu.VMEM((row_blocks, rows_count, RB), F32),
+            pltpu.VMEM((row_blocks, rows_count, CB), F32),
+            pltpu.VMEM((distinct, 8, CB), F32),
             pltpu.SMEM((rows_count, 8, wide), jnp.int32),
             pltpu.VMEM((ITERS, distinct + 8, CB), F32),
             pltpu.VMEM((ITERS, rows_count, distinct + 8, CB), F32),
@@ -365,30 +414,27 @@
         ),
         name="assign",
     )(groups, centroids.reshape(list_blocks, CB, D), row_weight.reshape(-1, 128),
-      id_message, id_column, use_table, live_table)
+      block_ids, count_table)
     out, load = pl.pallas_call(
         combine_kernel,
-        grid=(list_blocks,),
         out_shape=(
-            jax.ShapeDtypeStruct((list_blocks * CB, D), F32),
+            jax.ShapeDtypeStruct((list_blocks, CB, D), F32),
             jax.ShapeDtypeStruct((list_blocks, CB), F32),
         ),
-        in_specs=[
-            pl.BlockSpec(memory_space=pltpu.SMEM),
-            pl.BlockSpec((rows_count, USE * CB, D), lambda block: (0, 0, 0)),
-            pl.BlockSpec((rows_count, 8, CB), lambda block: (0, 0, 0)),
-            pl.BlockSpec((8, CB), lambda block: (0, 0)),
+        in_specs=[any_space, any_space, any_space],
+        out_specs=(any_space, vmem),
+        scratch_shapes=[
+            pltpu.VMEM((rows_count, USE * CB, D), BF16),
+            pltpu.VMEM((rows_count, 8, CB), F32),
+            pltpu.SMEM((rows_count, 8, wide), jnp.int32),
+            pltpu.VMEM((list_blocks, CB, D), F32),
+            dma((2 + rows_count,)),
+            dma((list_blocks,)),
         ],
-        out_specs=(
-            pl.BlockSpec((CB, D), lambda block: (block, 0)),
-            pl.BlockSpec((list_blocks, CB), lambda block: (0, 0)),
-        ),
-        compiler_params=pltpu.CompilerParams(
-            dimension_semantics=("arbitrary",), vmem_limit_bytes=48 * 2**20
-        ),
+        compiler_params=pltpu.CompilerParams(vmem_limit_bytes=56 * 2**20),
         name="combine",
-    )(all_ids, sums, mass, target)
-    return out, load.reshape(-1)
+    )(sums, mass, all_ids)
+    return out.reshape(-1, D), load.reshape(-1)
 
 
 def solution(mesh):

time: 251 us -> 242 us (0.964)
  local copies, waits for them, and re-layouts: 7.27 us -> 1.32 us
    unnamed x8 -> x0, local copies, waits for them, and re-layouts: 4.38 us -> none
    pallas_call x1, Pallas kernels: 9.82 us -> 6.36 us  [body(): pl.pallas_call(combine_kernel, out_shape=(jax.ShapeDtypeStruct((list_bloc...]
    pallas_call x1, Pallas kernels: 231 us -> 233 us  [body(): pl.pallas_call(functools.partial(main_kernel, rows_count, cents_count, li...]
where the time goes in v2:
time: 242 us
  Pallas kernels  240 us (99%)
    pallas_call x1, Pallas kernels, body(): pl.pallas_call(functools.partial(main_kernel, rows_count, cents_count, li...  233 us
    pallas_call x1, Pallas kernels, body(): pl.pallas_call(combine_kernel, out_shape=(jax.ShapeDtypeStruct((list_bloc...  6.36 us

profile of v2, /device:TPU:0, one launch (start us, length us, event | category | flops | bytes accessed | tf_op | source)
XLA Modules:
  0.0 241.6 jit_solution(6021464478258719475)
XLA Ops:
  0.6 1.3 broadcast_in_dim.2.block_counts
  1.9 233.3 %assign.1 = (bf16[8,256,1024]{2,1,0:T(8,128)(2,1)}, f32[8,8,128]{2,1,0:T(8,128)}, s32[8,8,128]{2,1,0:T(8,128)}) custom-call(bf16[2048,1024]{1,0:T(8,128)(2,1)} %groups.1, bf16[16,128,1024]{2,1,0:T(8,128)(2,1)} %bitcast.5, f32[16,128]{1,0:T(8,128)} %bitcast.6, s32[8,8]{1,0:T(8,128)} %block_ids.1, s32[8,8]{1,0:T(8,128)} %broadcast_in_dim.2.block_counts), custom_call_target="tpu_custom_call" | custom-call | flops 17179869184 | bytes 16777216 | tf_op jit(solution)/shard_map/assign/pallas_call | solution.py:369
  235.3 6.4 %combine.1 = (f32[16,128,1024]{2,1,0:T(8,128)}, f32[16,128]{1,0:T(8,128)}) custom-call(bf16[8,256,1024]{2,1,0:T(8,128)(2,1)} %get-tuple-element.7.sums, f32[8,8,128]{2,1,0:T(8,128)} %get-tuple-element.8.mass, s32[8,8,128]{2,1,0:T(8,128)} %get-tuple-element.9.ids), custom_call_target="tpu_custom_call" | custom-call | tf_op jit(solution)/shard_map/combine/pallas_call | solution.py:418

commit v3 on v2

--- a/solution.py
+++ b/solution.py
@@ -75,7 +75,11 @@
 
     ids = block_ids[...]
     slot = lax.broadcasted_iota(jnp.int32, ids.shape, 1)
-    alive = slot < block_counts[...]
+    block_row = lax.broadcasted_iota(jnp.int32, ids.shape, 0)
+    count = jnp.zeros(ids.shape, jnp.int32)
+    for block in range(row_blocks):
+        count = jnp.where(block_row == block, block_counts[block], count)
+    alive = slot < count
     place = lax.broadcasted_iota(jnp.int32, id_message.shape, 1) % distinct
     message = jnp.zeros(id_message.shape, jnp.int32)
     for j in range(rows_count):
@@ -118,7 +122,7 @@
     ]
     for copy in id_copies:
         copy.wait_recv()
-    to_scalar = pltpu.make_async_copy(ids_out, ids_scalar, load_sem.at[2])
+    to_scalar = pltpu.make_async_copy(ids_out.at[:, 0:1, :], ids_scalar, load_sem.at[2])
     to_scalar.start()
     to_scalar.wait()
     load_lists.wait()
@@ -134,10 +138,11 @@
             send.at[j], lists_in.at[j], list_send_sem.at[j], list_recv_sem.at[j], peers[j]
         )
 
-    for j in far[:1] + near + far[1:]:
+    ahead = 2
+    for j in far[:ahead] + near + far[ahead:]:
         for use in range(USE):
             send[j, use * CB : (use + 1) * CB, :] = normalized_list(j, use)
-        if j in near or j == far[0]:
+        if j in near or j in far[:ahead]:
             start_lists(j)
     own_ids = [lax.rem(ids_scalar[0, 0, use], list_blocks) for use in range(USE)]
     for use in range(USE):
@@ -191,8 +196,8 @@
         scores_of(j)
     for index, j in enumerate(far):
         list_copies[j].wait_send()
-        if index + 1 < len(far):
-            start_lists(far[index + 1])
+        if index + ahead < len(far):
+            start_lists(far[index + ahead])
         list_copies[j].wait_recv()
         scores_of(j)
 
@@ -312,7 +317,7 @@
     rows_count = sums.shape[0]
     list_blocks = load.shape[0]
     copies = [
-        pltpu.make_async_copy(ids, ids_scalar, in_sem.at[0]),
+        pltpu.make_async_copy(ids.at[:, 0:1, :], ids_scalar, in_sem.at[0]),
         pltpu.make_async_copy(mass, mass_here, in_sem.at[1]),
     ]
     copies += [
@@ -361,7 +366,6 @@
     list_total = list_blocks * CB * rows_count * cents_count
     distinct = rows_count * USE
     wide = rows_count * distinct
-    count_table = jnp.broadcast_to(block_counts[:, None], block_ids.shape)
     any_space = pl.BlockSpec(memory_space=pl.ANY)
     vmem = pl.BlockSpec(memory_space=pltpu.VMEM)
     dma = pltpu.SemaphoreType.DMA
@@ -373,7 +377,7 @@
             jax.ShapeDtypeStruct((rows_count, 8, CB), F32),
             jax.ShapeDtypeStruct((rows_count, 8, wide), jnp.int32),
         ),
-        in_specs=[any_space, any_space, vmem, vmem, vmem],
+        in_specs=[any_space, any_space, vmem, vmem, pl.BlockSpec(memory_space=pltpu.SMEM)],
         out_specs=(any_space, vmem, vmem),
         scratch_shapes=[
             pltpu.VMEM((row_total, D), BF16),
@@ -389,7 +393,7 @@
             pltpu.VMEM((row_blocks, rows_count, RB), F32),
             pltpu.VMEM((row_blocks, rows_count, CB), F32),
             pltpu.VMEM((distinct, 8, CB), F32),
-            pltpu.SMEM((rows_count, 8, wide), jnp.int32),
+            pltpu.SMEM((rows_count, 1, wide), jnp.int32),
             pltpu.VMEM((ITERS, distinct + 8, CB), F32),
             pltpu.VMEM((ITERS, rows_count, distinct + 8, CB), F32),
             pltpu.VMEM((distinct, CB), F32),
@@ -414,7 +418,7 @@
         ),
         name="assign",
     )(groups, centroids.reshape(list_blocks, CB, D), row_weight.reshape(-1, 128),
-      block_ids, count_table)
+      block_ids, block_counts)
     out, load = pl.pallas_call(
         combine_kernel,
         out_shape=(
@@ -426,7 +430,7 @@
         scratch_shapes=[
             pltpu.VMEM((rows_count, USE * CB, D), BF16),
             pltpu.VMEM((rows_count, 8, CB), F32),
-            pltpu.SMEM((rows_count, 8, wide), jnp.int32),
+            pltpu.SMEM((rows_count, 1, wide), jnp.int32),
             pltpu.VMEM((list_blocks, CB, D), F32),
             dma((2 + rows_count,)),
             dma((list_blocks,)),

time: 242 us -> 229 us (0.946)
  Pallas kernels: 240 us -> 229 us
    pallas_call x1, Pallas kernels: 233 us -> 222 us  [body(): pl.pallas_call(functools.partial(main_kernel, rows_count, cents_count, li...]
where the time goes in v3:
time: 229 us
  Pallas kernels  229 us (100%)
    pallas_call x1, Pallas kernels, body(): pl.pallas_call(functools.partial(main_kernel, rows_count, cents_count, li...  222 us
    pallas_call x1, Pallas kernels, body(): pl.pallas_call(combine_kernel, out_shape=(jax.ShapeDtypeStruct((list_bloc...  6.35 us

profile of v3, /device:TPU:0, one launch (start us, length us, event | category | flops | bytes accessed | tf_op | source)
XLA Modules:
  0.0 229.2 jit_solution(7477866778627051962)
XLA Ops:
  0.6 222.2 %assign.1 = (bf16[8,256,1024]{2,1,0:T(8,128)(2,1)}, f32[8,8,128]{2,1,0:T(8,128)}, s32[8,8,128]{2,1,0:T(8,128)}) custom-call(bf16[2048,1024]{1,0:T(8,128)(2,1)} %groups.1, bf16[16,128,1024]{2,1,0:T(8,128)(2,1)} %bitcast.5, f32[16,128]{1,0:T(8,128)} %bitcast.6, s32[8,8]{1,0:T(8,128)} %block_ids.1, s32[8]{0:T(128)} %block_counts.1), custom_call_target="tpu_custom_call" | custom-call | flops 17179869184 | bytes 16777216 | tf_op jit(solution)/shard_map/assign/pallas_call | solution.py:373
  222.8 6.3 %combine.1 = (f32[16,128,1024]{2,1,0:T(8,128)}, f32[16,128]{1,0:T(8,128)}) custom-call(bf16[8,256,1024]{2,1,0:T(8,128)(2,1)} %get-tuple-element.7.sums, f32[8,8,128]{2,1,0:T(8,128)} %get-tuple-element.8.mass, s32[8,8,128]{2,1,0:T(8,128)} %get-tuple-element.9.ids), custom_call_target="tpu_custom_call" | custom-call | tf_op jit(solution)/shard_map/combine/pallas_call | solution.py:422

commit v4 on v3

--- a/solution.py
+++ b/solution.py
@@ -15,7 +15,6 @@
 BETA = 32.0
 EPSILON = 1e-06
 PRIOR = 0.25
-HIGHEST = lax.Precision.HIGHEST
 MESH = pl.DeviceIdType.MESH
 F32 = jnp.float32
 BF16 = jnp.bfloat16
@@ -138,7 +137,7 @@
             send.at[j], lists_in.at[j], list_send_sem.at[j], list_recv_sem.at[j], peers[j]
         )
 
-    ahead = 2
+    ahead = max(len(far) - 1, 1)
     for j in far[:ahead] + near + far[ahead:]:
         for use in range(USE):
             send[j, use * CB : (use + 1) * CB, :] = normalized_list(j, use)
@@ -161,12 +160,14 @@
         spread = jnp.broadcast_to(weights[index : index + 1, :], (128, 128))
         weight_column[index * 128 : (index + 1) * 128, :] = spread.T
 
-    wide = match.shape[1]
+    wide = id_column.shape[1]
     lane = lax.broadcasted_iota(jnp.int32, (1, wide), 1)
     id_row = jnp.zeros((1, wide), jnp.int32)
     for j in range(rows_count):
         id_row = id_row + jnp.where(lane // distinct == j, ids_out[j, 0:1, :], 0)
-    match[...] = (id_column[...] == id_row).astype(F32)
+    same = (id_column[...] == id_row).astype(F32).astype(BF16)
+    for term in range(3):
+        match[:, term * wide : (term + 1) * wide] = same
 
     for copy in weight_copies:
         copy.wait_recv()
@@ -224,7 +225,7 @@
             return carry
 
         column_parts[...] = jnp.zeros_like(column_parts)
-        lax.fori_loop(0, row_blocks, column_step, 0, unroll=2)
+        lax.fori_loop(0, row_blocks, column_step, 0, unroll=4)
         parts[step, :distinct, :] = jnp.sum(column_parts[...], axis=1)
         copies = [
             remote(
@@ -242,10 +243,13 @@
             for j in range(1, rows_count):
                 mass = mass + parts_in[0, j, distinct : distinct + 8, :]
             total[...] = mass / list_total
+        arrived = parts_in[step, :, :distinct, :].reshape(rows_count * distinct, CB)
+        first = arrived.astype(BF16)
+        rest = arrived - first.astype(F32)
+        second = rest.astype(BF16)
+        third = (rest - second.astype(F32)).astype(BF16)
         column_all = jnp.dot(
-            match[...],
-            parts_in[step, :, :distinct, :].reshape(rows_count * distinct, CB),
-            precision=HIGHEST, preferred_element_type=F32,
+            match[...], jnp.concatenate([first, second, third], axis=0), preferred_element_type=F32
         )
         target = total[0:1, :]
         scales[...] = target / (column_all + PRIOR * target)
@@ -255,7 +259,7 @@
         row_scale[where, :] = row_step(block)
         return carry
 
-    lax.fori_loop(0, row_blocks, last_rows, 0, unroll=2)
+    lax.fori_loop(0, row_blocks, last_rows, 0, unroll=4)
 
     sum_copies = []
     mass_copies = []
@@ -397,7 +401,7 @@
             pltpu.VMEM((ITERS, distinct + 8, CB), F32),
             pltpu.VMEM((ITERS, rows_count, distinct + 8, CB), F32),
             pltpu.VMEM((distinct, CB), F32),
-            pltpu.VMEM((distinct, wide), F32),
+            pltpu.VMEM((distinct, 3 * wide), BF16),
             pltpu.VMEM((rows_count, 8, CB), F32),
             pltpu.VMEM((8, CB), F32),
             pltpu.VMEM((cents_count, 8, CB), F32),

time: 229 us -> 226 us (0.987)
  Pallas kernels: 229 us -> 225 us
    pallas_call x1, Pallas kernels: 222 us -> 219 us  [body(): pl.pallas_call(functools.partial(main_kernel, rows_count, cents_count, li...]
where the time goes in v4:
time: 226 us
  Pallas kernels  225 us (100%)
    pallas_call x1, Pallas kernels, body(): pl.pallas_call(functools.partial(main_kernel, rows_count, cents_count, li...  219 us
    pallas_call x1, Pallas kernels, body(): pl.pallas_call(combine_kernel, out_shape=(jax.ShapeDtypeStruct((list_bloc...  6.34 us

profile of v4, /device:TPU:0, one launch (start us, length us, event | category | flops | bytes accessed | tf_op | source)
XLA Modules:
  0.0 225.8 jit_solution(15062984266842757913)
XLA Ops:
  0.6 218.8 %assign.1 = (bf16[8,256,1024]{2,1,0:T(8,128)(2,1)}, f32[8,8,128]{2,1,0:T(8,128)}, s32[8,8,128]{2,1,0:T(8,128)}) custom-call(bf16[2048,1024]{1,0:T(8,128)(2,1)} %groups.1, bf16[16,128,1024]{2,1,0:T(8,128)(2,1)} %bitcast.5, f32[16,128]{1,0:T(8,128)} %bitcast.6, s32[8,8]{1,0:T(8,128)} %block_ids.1, s32[8]{0:T(128)} %block_counts.1), custom_call_target="tpu_custom_call" | custom-call | flops 17179869184 | bytes 16777216 | tf_op jit(solution)/shard_map/assign/pallas_call | solution.py:377
  219.4 6.3 %combine.1 = (f32[16,128,1024]{2,1,0:T(8,128)}, f32[16,128]{1,0:T(8,128)}) custom-call(bf16[8,256,1024]{2,1,0:T(8,128)(2,1)} %get-tuple-element.7.sums, f32[8,8,128]{2,1,0:T(8,128)} %get-tuple-element.8.mass, s32[8,8,128]{2,1,0:T(8,128)} %get-tuple-element.9.ids), custom_call_target="tpu_custom_call" | custom-call | tf_op jit(solution)/shard_map/combine/pallas_call | solution.py:426

commit v5 on v4

--- a/solution.py
+++ b/solution.py
@@ -137,7 +137,7 @@
             send.at[j], lists_in.at[j], list_send_sem.at[j], list_recv_sem.at[j], peers[j]
         )
 
-    ahead = max(len(far) - 1, 1)
+    ahead = len(far)
     for j in far[:ahead] + near + far[ahead:]:
         for use in range(USE):
             send[j, use * CB : (use + 1) * CB, :] = normalized_list(j, use)

time: 226 us -> 226 us (level)
  no operation moved by 1% of the time
where the time goes in v5:
time: 226 us
  Pallas kernels  225 us (100%)
    pallas_call x1, Pallas kernels, body(): pl.pallas_call(functools.partial(main_kernel, rows_count, cents_count, li...  219 us
    pallas_call x1, Pallas kernels, body(): pl.pallas_call(combine_kernel, out_shape=(jax.ShapeDtypeStruct((list_bloc...  6.34 us

profile of v5, /device:TPU:0, one launch (start us, length us, event | category | flops | bytes accessed | tf_op | source)
XLA Modules:
  0.0 225.9 jit_solution(14948331007402315879)
XLA Ops:
  0.6 218.9 %assign.1 = (bf16[8,256,1024]{2,1,0:T(8,128)(2,1)}, f32[8,8,128]{2,1,0:T(8,128)}, s32[8,8,128]{2,1,0:T(8,128)}) custom-call(bf16[2048,1024]{1,0:T(8,128)(2,1)} %groups.1, bf16[16,128,1024]{2,1,0:T(8,128)(2,1)} %bitcast.5, f32[16,128]{1,0:T(8,128)} %bitcast.6, s32[8,8]{1,0:T(8,128)} %block_ids.1, s32[8]{0:T(128)} %block_counts.1), custom_call_target="tpu_custom_call" | custom-call | flops 17179869184 | bytes 16777216 | tf_op jit(solution)/shard_map/assign/pallas_call | solution.py:377
  219.5 6.3 %combine.1 = (f32[16,128,1024]{2,1,0:T(8,128)}, f32[16,128]{1,0:T(8,128)}) custom-call(bf16[8,256,1024]{2,1,0:T(8,128)(2,1)} %get-tuple-element.7.sums, f32[8,8,128]{2,1,0:T(8,128)} %get-tuple-element.8.mass, s32[8,8,128]{2,1,0:T(8,128)} %get-tuple-element.9.ids), custom_call_target="tpu_custom_call" | custom-call | tf_op jit(solution)/shard_map/combine/pallas_call | solution.py:426
